TPU v7x, 128 devices: a whole 4x4x4 slice. The times are simulated.
128 devices in a mesh: owner: 8 (over y_hi, z), dp: 16 (over x, y_lo, core).
Axes of the slice: x: 4, y: 4 (y_hi: 2, y_lo: 2; y = y_hi * 2 + y_lo), z: 4, core: 2. Of those that a mesh axis runs over, the one named last changes fastest.
Arguments:
- query_grad: bfloat16 [1024, 16384], P('dp', 'owner'), may hold values from -6 to 6
- query_act: bfloat16 [1024, 8192], P('dp'), may hold values from -6 to 6
- train_grad: bfloat16 [8192, 16384], P('dp', 'owner'), may hold values from -6 to 6
- train_act: bfloat16 [8192, 8192], P('dp'), may hold values from -6 to 6
- basis_out: bfloat16 [16384, 512], P('owner'), may hold values from -0.25 to 0.25
- basis_in: bfloat16 [8192, 512], P('dp'), may hold values from -0.25 to 0.25
- eigenvalues: float32 [16384, 8192], P('owner', 'dp'), may hold values from 0.1 to 10
Outputs:
- token_scores: float32 [8192], P('dp')
- influence: float32 [128], P('dp')
All inputs are finite; a program needn't handle non-finite values.
Results may differ from a plain program's by a relative error of at most 0.0065.
Values may be sent and summed in bfloat16 or wider, within the bound.
A program may use at most 192 MiB of HBM per device.

v0:
```python
import math

import jax
import jax.numpy as jnp
from jax import lax
from jax.sharding import PartitionSpec as P

DIN = 8192
DOUT = 16384
SEQ_LEN = 64


def rotate_rows(rows, basis):
    count, width = rows.shape
    size = basis.shape[1]
    parts = rows.reshape(count, width // size, size)
    blocks = basis.reshape(width // size, size, size)
    return jnp.einsum("tkr,krc->tkc", parts, blocks, preferred_element_type=jnp.float32).reshape(
        count, width
    )


def on_device(query_grad, query_act, train_grad, train_act, basis_out, basis_in, eigenvalues):
    act_cols = lax.all_to_all(query_act, "dp", split_axis=1, concat_axis=0, tiled=True)
    act_rot = rotate_rows(act_cols, basis_in).astype(jnp.bfloat16)
    local_rot = rotate_rows(query_grad, basis_out).astype(jnp.bfloat16)
    grad_rot = lax.all_gather(local_rot, "dp", axis=0, tiled=True)
    total_query = grad_rot.shape[0]
    cross = lax.dot_general(
        grad_rot, act_rot, (((0,), (0,)), ((), ())), preferred_element_type=jnp.float32
    )
    scaled = (cross / (math.sqrt(total_query) * eigenvalues)).astype(jnp.bfloat16)
    unit_rows, feat_cols = scaled.shape
    size = basis_out.shape[1]
    out_blocks = basis_out.reshape(unit_rows // size, size, size)
    half = jnp.einsum(
        "krc,kcj->krj",
        out_blocks,
        scaled.reshape(unit_rows // size, size, feat_cols),
        preferred_element_type=jnp.float32,
    )
    half = half.reshape(unit_rows, feat_cols).astype(jnp.bfloat16)
    in_blocks = basis_in.reshape(feat_cols // size, size, size)
    precond = jnp.einsum(
        "imc,mjc->imj",
        half.reshape(unit_rows, feat_cols // size, size),
        in_blocks,
        preferred_element_type=jnp.float32,
    )
    precond = precond.reshape(unit_rows, feat_cols).astype(jnp.bfloat16)
    local_tokens = train_act.shape[0]
    image = lax.dot_general(
        train_act,
        lax.all_gather(precond, "dp", axis=1, tiled=True),
        (((1,), (1,)), ((), ())),
        preferred_element_type=jnp.float32,
    )
    partial_value = jnp.sum(train_grad.astype(jnp.float32) * image, axis=1)
    scores = lax.psum(partial_value, "owner")
    token_scores = scores / math.sqrt(DOUT * DIN)
    influence = jnp.mean(token_scores.reshape(local_tokens // SEQ_LEN, SEQ_LEN), axis=1)
    return (token_scores, influence)


def solution(mesh):
    placed = (
        P("dp", "owner"),
        P("dp", None),
        P("dp", "owner"),
        P("dp", None),
        P("owner", None),
        P("dp", None),
        P("owner", "dp"),
    )
    return jax.shard_map(
        on_device, mesh=mesh, in_specs=placed, out_specs=(P("dp"), P("dp")), check_vma=False
    )
```

profile of v0, /device:TPU:0, one launch (start us, length us, event | category | flops | bytes accessed | tf_op | source)
XLA Modules:
  0.0 299.6 jit_solution(14178932645792022799)
XLA Ops:
  7.2 0.0 copy-start
  7.2 0.0 all-gather.3.cloned.1.call-start
  7.2 1.5 copy-done
  8.8 1.4 fusion.2
  10.2 0.7 copy.28
  10.9 0.0 all-gather.3.cloned.1.call-update
  10.9 0.0 all-gather.5.cloned.1.call-start
  11.0 1.3 copy.34
  12.3 25.6 %all_to_all.16 = bf16[64,16,512]{2,0,1:T(8,128)(2,1)S(1)} all-to-all(bf16[64,16,512]{2,0,1:T(8,128)(2,1)S(1)} %bitcast.44), channel_id=1, replica_groups=mesh['owner'=8,'dp'=16] {'dp'}, dimensions={1} | all-to-all | bytes 2097152 | tf_op jit(solution)/shard_map/all_to_all | solution.py:24
  37.9 20.0 %all-gather.3.cloned.1.call-done = bf16[1024,2048]{1,0:T(8,128)(2,1)} async-done(((bf16[64,2048]{1,0:T(8,128)(2,1)}), bf16[1024,2048]{1,0:T(8,128)(2,1)}) %all-gather.3.cloned.1.call-update) | async-done | bytes 4194320 | tf_op jit(solution)/shard_map/all_gather | solution.py:27
  57.9 8.1 %divide_convert_fusion = bf16[2048,512]{1,0:T(8,128)(2,1)} fusion(f32[2048,512]{1,0:T(8,128)} %param.13, bf16[1024,2048]{1,0:T(8,128)(2,1)} %all-gather.3.cloned.1.call-done, bf16[512,512]{1,0:T(8,128)(2,1)} %param.12, bf16[1024,512]{1,0:T(8,128)(2,1)S(1)} %bitcast.46), kind=kOutput, calls=%fused_computation.2 | convolution fusion | flops 2688024576 | bytes 12058624 | tf_op jit(solution)/shard_map/dot_general | solution.py:29
  66.0 0.0 copy-start.4
  66.0 2.9 convolution_convert_fusion.1
  68.9 0.0 copy-done.4
  68.9 0.0 copy-start.2
  68.9 2.7 convolution_convert_fusion
  71.6 0.0 all-gather.5.cloned.1.call-update
  71.6 0.0 copy-done.2
  71.7 2.5 copy.22
  74.2 168.7 %all-gather.5.cloned.1.call-done = bf16[2048,8192]{1,0:T(8,128)(2,1)} async-done(((bf16[2048,512]{1,0:T(8,128)(2,1)}), bf16[2048,8192]{1,0:T(8,128)(2,1)}) %all-gather.5.cloned.1.call-update) | async-done | bytes 33554448 | tf_op jit(solution)/shard_map/all_gather | solution.py:54
  242.9 0.0 copy-start.1
  242.9 25.0 %fusion = f32[512]{0:T(512)S(1)} fusion(bf16[512,2048]{0,1:T(8,128)(2,1)} %copy.22, bf16[2048,8192]{1,0:T(8,128)(2,1)} %all-gather.5.cloned.1.call-done, bf16[512,8192]{1,0:T(8,128)(2,1)} %param.10), kind=kOutput, calls=%fused_computation.1 | convolution fusion | flops 17183014912 | bytes 44042240 | tf_op jit(solution)/shard_map/dot_general | solution.py:52
  267.9 24.1 %psum.7 = f32[512]{0:T(512)S(1)} all-reduce(f32[512]{0:T(512)S(1)} %fusion), channel_id=1, replica_groups=mesh['owner'=8,'dp'=16] {'owner'}, use_global_device_ids=true, to_apply=%region_1.0 | all-reduce | flops 512 | bytes 4096 | tf_op jit(solution)/shard_map/psum | solution.py:59
  292.0 0.0 copy-start.3
  292.0 0.1 reshape.50
  292.1 0.1 reduce_sum.19
  292.2 0.5 broadcast_multiply_fusion.1
  292.7 0.0 copy-done.3
  292.7 0.0 copy-done.1
  (1 shorter events, 0.0 us)
Async XLA Ops:
  7.2 1.6 copy-start
  7.2 50.7 %all-gather.3.cloned.1.call-start = ((), (), s32[]{:S(2)}) async-start(), calls=%async_computation.1 | async-start | bytes 4456448 | tf_op jit(solution)/shard_map/all_gather | solution.py:27
  10.9 232.0 %all-gather.5.cloned.1.call-start = ((), (), s32[]{:S(2)}) async-start(), calls=%async_computation.2 | async-start | bytes 35651584 | tf_op jit(solution)/shard_map/all_gather | solution.py:54
  66.0 2.9 copy-start.4
  68.9 2.7 copy-start.2
  242.9 49.8 %copy-start.1 = (bf16[2048,512]{1,0:T(8,128)(2,1)S(1)}, bf16[2048,512]{1,0:T(8,128)(2,1)}, u32[]{:S(2)}) copy-start(bf16[2048,512]{1,0:T(8,128)(2,1)} %param.11) | copy-start | bytes 6291460
  292.0 0.7 copy-start.3
Sparse Core Ops, SparseCore 0:
  11.0 46.8 all-gather.2
  71.8 171.1 all-gather.4
where the time goes:
time: 300 us
  waiting for transfers between devices  189 us (63%)
  blocking collectives  49.6 us (17%)
  matrix products  40.1 us (13%)
  between operations  14.1 us (5%)
  local copies, waits for them, and re-layouts  6.21 us (2%)
    all_gather x1, waiting for transfers between devices, on_device(): lax.all_gather(precond, 'dp', axis=1, tiled=True)  169 us
    all_to_all x1, blocking collectives, on_device(): lax.all_to_all(query_act, 'dp', split_axis=1, concat_axis=0, tiled=True)  25.6 us
    dot_general x1, matrix products, on_device(): lax.dot_general(train_act, lax.all_gather(precond, 'dp', axis=1, tiled=Tr...  25 us
    psum x1, blocking collectives, on_device(): scores = lax.psum(partial_value, 'owner')  24.1 us
    all_gather x1, waiting for transfers between devices, on_device(): grad_rot = lax.all_gather(local_rot, 'dp', axis=0, tiled=True)  20 us
    dot_general x1, matrix products, on_device(): lax.dot_general(grad_rot, act_rot, (((0,), (0,)), ((), ())), preferred_el...  8.08 us
  transfers between devices with their start and end apart: 2, of which 2 were waited for; matrix products, arithmetic and copies ran while one was open for 1% of the time, Pallas kernels for 0%

commit v1 on v0

v1 whole, which is shorter than its diff:
```python
import math

import jax
import jax.numpy as jnp
from jax import lax
from jax.experimental import pallas as pl
from jax.experimental.pallas import tpu as pltpu
from jax.sharding import PartitionSpec as P

DIN = 8192
DOUT = 16384
SEQ_LEN = 64
EB = 512
QTOK = 1024
MESH = pl.DeviceIdType.MESH
F32 = jnp.float32
BF16 = jnp.bfloat16


def mm(a, b, ca=1, cb=0):
    return lax.dot_general(a, b, (((ca,), (cb,)), ((), ())), preferred_element_type=F32)


def kernel(qg, qa, tg, ta, uo, ui, lam, out, qg_v, uo_v, ui_v, lam_v, rlt, gr, ac, art, gb, ab, a_st, pt, acc,
           part, r1, r2, ssem, lsem, ac_s, gr_s, art_s, ab_s, az_s, asib_s, gsem, p_s, r1_s, r2_s):
    dp, ow = lax.axis_index("dp"), lax.axis_index("owner")
    x, yl, c = dp // 4, (dp // 2) % 2, dp % 2
    yh, z = ow // 4, ow % 4
    xr, xl, x2 = (x + 1) % 4, (x + 3) % 4, (x + 2) % 4
    me4 = yl * 2 + c

    def d_of(x_, yl_, c_):
        return (x_ * 2 + yl_) * 2 + c_

    right = (ow, d_of(xr, yl, c))
    left = (ow, d_of(xl, yl, c))
    sib = (ow, d_of(x, yl, 1 - c))
    across = (ow, d_of(x, 1 - yl, c))
    diag = (ow, d_of(x, 1 - yl, 1 - c))
    bnb = ((1 - yh) * 4 + z, d_of(x, 1 - yl, c))
    zs = [(yh * 4 + (z + k) % 4, dp) for k in (1, 3, 2)]
    owners = [((ow + k) % 8, dp) for k in range(1, 8)]
    dps = [(ow, (dp + k) % 16) for k in range(1, 16)]

    bar = pltpu.get_barrier_semaphore()
    peers = dps + owners + [bnb]
    for p in peers:
        pl.semaphore_signal(bar, inc=1, device_id=p, device_id_type=MESH)

    sends, locs = [], []

    def send(src, dst, rsem, to):
        cp = pltpu.make_async_remote_copy(src, dst, ssem.at[len(sends)], rsem, device_id=to, device_id_type=MESH)
        cp.start()
        sends.append(cp)

    def got(region, rsem):
        pltpu.make_async_remote_copy(region, region, ssem.at[0], rsem, device_id=sib, device_id_type=MESH).wait_recv()

    def local(src, dst):
        cp = pltpu.make_async_copy(src, dst, lsem.at[len(locs)])
        cp.start()
        locs.append(cp)
        return cp

    def cols(x_, yl_, c_):
        return pl.ds(pl.multiple_of(x_ * 2048 + yl_ * 1024 + c_ * 512, 512), 512)

    l_qg = local(qg, qg_v)
    l_uo = local(uo, uo_v)
    l_ui = local(ui, ui_v)
    q16 = pl.ds(pl.multiple_of(z * 16, 16), 16)
    l_ac = local(qa.at[q16, pl.ds(pl.multiple_of(dp * 512, 512), 512)], ac.at[dp])
    l_lam = local(lam, lam_v)

    l_qg.wait()
    l_uo.wait()
    for k in range(4):
        rot = mm(qg_v[:, k * 512:(k + 1) * 512], uo_v[k * 512:(k + 1) * 512, :])
        gr[k, :, dp, :, :] = rot.astype(BF16).reshape(4, 16, 512)

    pl.semaphore_wait(bar, len(peers))

    for to in dps:
        send(qa.at[q16, pl.ds(pl.multiple_of(to[1] * 512, 512), 512)], ac.at[dp], ac_s, to)

    def gblock(d, h):
        return gr.at[pl.ds(2 * h, 2), :, d]

    def gsend(d, h, to):
        send(gblock(d, h), gblock(d, h), gr_s.at[d, h], to)

    def ggot(d, h):
        got(gblock(d, h), gr_s.at[d, h])

    for h in range(2):
        for to in (right, left, across, sib):
            gsend(dp, h, to)

    z128 = pl.ds(pl.multiple_of(z * 128, 128), 128)
    for k in range(4):
        at = slice(k * 512, (k + 1) * 512)
        send(ta.at[z128, cols(k, 1 - yl, 1 - c)], a_st.at[:, at], ab_s.at[1], bnb)
    for k in range(4):
        at = slice(k * 512, (k + 1) * 512)
        send(ta.at[z128, cols(k, 1 - yl, c)], ab.at[me4, z128, at], ab_s.at[0], bnb)

    def recip(k):
        rlt[k] = (1.0 / (math.sqrt(QTOK) * lam_v[k * 512:(k + 1) * 512, :])).T

    l_lam.wait()
    recip(0)

    l_ui.wait()
    l_ac.wait()
    got(ac.at[pl.ds(0, 15)], ac_s)
    art[z] = mm(ac[...].reshape(256, 512), ui_v[...]).T.astype(BF16)
    for to in zs:
        send(art.at[z], art.at[z], art_s.at[z], to)

    dl, dr, da = d_of(xl, yl, c), d_of(xr, yl, c), d_of(x, 1 - yl, c)
    for h in range(2):
        ggot(da, h)
        gsend(da, h, right)
        gsend(da, h, left)
        ggot(dl, h)
        if h == 0:
            gsend(dl, h, right)
        ggot(dr, h)
        if h == 1:
            gsend(dr, h, left)
        for d in (da, dl, dr):
            gsend(d, h, sib)
    recip(1)
    for h in range(2):
        d2 = d_of(x2, yl, c)
        ggot(d2, h)
        gsend(d2, h, across)
        gsend(d2, h, sib)
    for h in range(2):
        for x_ in (xl, xr):
            d = d_of(x_, 1 - yl, c)
            ggot(d, h)
            gsend(d, h, sib)
    for h in range(2):
        d = d_of(x2, 1 - yl, c)
        ggot(d, h)
        gsend(d, h, sib)

    send(tg, gb.at[me4], gsem.at[me4], across)
    send(tg, gb.at[me4], gsem.at[me4], sib)
    for k in range(4):
        send(ta.at[:, cols(k, yl, 1 - c)], ab.at[me4, :, k * 512:(k + 1) * 512], asib_s.at[0], sib)
    l_g = local(tg, gb.at[me4])
    l_a = [local(ta.at[:, cols(k, yl, c)], ab.at[me4, :, k * 512:(k + 1) * 512]) for k in range(4)]

    s_ac, s_ad = (1 - yl) * 2 + c, (1 - yl) * 2 + 1 - c
    got(a_st, ab_s.at[1])
    send(a_st, ab.at[s_ac, z128], asib_s.at[1], sib)
    got(ab.at[s_ac, z128], ab_s.at[0])
    for to in zs:
        send(ab.at[s_ac, z128], ab.at[s_ac, z128], az_s.at[0, z], to)
    got(ab.at[s_ad, z128], asib_s.at[1])
    for to in zs:
        send(ab.at[s_ad, z128], ab.at[s_ad, z128], az_s.at[1, z], to)

    recip(2)
    recip(3)
    for k in (1, 2, 3):
        z_ = (z + k) % 4
        got(art.at[z_], art_s.at[z_])

    def xrows(x_):
        return pl.ds(pl.multiple_of(x_ * 512, 512), 512)

    for k in range(4):
        if k % 2 == 0:
            for x_ in range(4):
                for y_ in range(2):
                    ggot(d_of(x_, y_, 1 - c), k // 2)
        cross = mm(art[0], gr[k, 0].reshape(256, 512))
        for z_ in range(1, 4):
            cross = cross + mm(art[z_], gr[k, z_].reshape(256, 512))
        scaled = (cross * rlt[k]).astype(BF16)
        half = mm(scaled, uo_v[k * 512:(k + 1) * 512, :], 1, 1).astype(BF16)
        pt[k, xrows(x), :] = mm(ui_v[...], half).astype(BF16)
        mine = pt.at[k, xrows(x)]
        send(mine, mine, p_s.at[k, 0], right)
        send(mine, mine, p_s.at[k, 1], left)

    acc[...] = jnp.zeros_like(acc)

    def image(k, tb):
        @pl.loop(0, 2)
        def _(r):
            rows = pl.ds(pl.multiple_of(r * 256, 256), 256)
            img = mm(ab[tb, rows, :], pt[k])
            prod = img * gb[tb, rows, k * 512:(k + 1) * 512].astype(F32)
            acc[tb, rows, :] += prod[:, :128] + prod[:, 128:256] + prod[:, 256:384] + prod[:, 384:]

    def relay(k):
        from_l = pt.at[k, xrows(xl)]
        got(from_l, p_s.at[k, 0])
        half0 = pt.at[k, pl.ds(pl.multiple_of(xl * 512, 512), 256)]
        send(half0, half0, p_s.at[k, 2], right)
        from_r = pt.at[k, xrows(xr)]
        got(from_r, p_s.at[k, 1])
        half1 = pt.at[k, pl.ds(pl.multiple_of(xr * 512 + 256, 256), 256)]
        send(half1, half1, p_s.at[k, 3], left)

    def p_all(k):
        got(pt.at[k, pl.ds(pl.multiple_of(x2 * 512, 512), 256)], p_s.at[k, 2])
        got(pt.at[k, pl.ds(pl.multiple_of(x2 * 512 + 256, 256), 256)], p_s.at[k, 3])

    relay(0)
    l_g.wait()
    for cp in l_a:
        cp.wait()
    got(gb.at[me4 + 1 - 2 * c], gsem.at[me4 + 1 - 2 * c])
    got(ab.at[me4 + 1 - 2 * c], asib_s.at[0])
    tb_own, tb_sib = me4, me4 + 1 - 2 * c
    relay(1)
    p_all(0)
    image(0, tb_own)
    image(0, tb_sib)
    relay(2)
    got(gb.at[s_ac], gsem.at[s_ac])
    send(gb.at[s_ac], gb.at[s_ac], gsem.at[s_ac], sib)
    p_all(1)
    image(1, tb_own)
    image(1, tb_sib)
    for k in (1, 2, 3):
        z_ = (z + k) % 4
        rows = pl.ds(pl.multiple_of(z_ * 128, 128), 128)
        got(ab.at[s_ac, rows], az_s.at[0, z_])
        got(ab.at[s_ad, rows], az_s.at[1, z_])
    got(gb.at[s_ad], gsem.at[s_ad])
    relay(3)
    for k in range(2):
        image(k, s_ac)
        image(k, s_ad)
    for k in range(2, 4):
        p_all(k)
        for tb in (tb_own, tb_sib, s_ac, s_ad):
            image(k, tb)

    for tb in range(4):
        part[tb] = jnp.sum(acc[tb].T, axis=0, keepdims=True)
    for to, slot in ((sib, tb_sib), (across, s_ac), (diag, s_ad)):
        send(part.at[slot], r1.at[me4], r1_s.at[me4], to)
    r1[me4] = part[me4]
    for slot in (tb_sib, s_ac, s_ad):
        got(r1.at[slot], r1_s.at[slot])
    r2[ow] = (r1[0] + r1[1]) + (r1[2] + r1[3])
    for to in owners:
        send(r2.at[ow], r2.at[ow], r2_s.at[ow], to)
    for o in owners:
        got(r2.at[o[0]], r2_s.at[o[0]])
    total = r2[0]
    for o in range(1, 8):
        total = total + r2[o]
    out[...] = total * (1.0 / math.sqrt(DOUT * DIN))
    for cp in sends:
        cp.wait_send()


def on_device(query_grad, query_act, train_grad, train_act, basis_out, basis_in, eigenvalues):
    dma, vmem = pltpu.SemaphoreType.DMA, pltpu.VMEM
    scores = pl.pallas_call(
        kernel,
        out_shape=jax.ShapeDtypeStruct((1, 512), F32),
        in_specs=[pl.BlockSpec(memory_space=pl.ANY)] * 7,
        out_specs=pl.BlockSpec(memory_space=pltpu.VMEM),
        scratch_shapes=[
            vmem((64, 2048), BF16),
            vmem((2048, 512), BF16),
            vmem((512, 512), BF16),
            vmem((2048, 512), F32),
            vmem((4, 512, 512), F32),
            vmem((4, 4, 16, 16, 512), BF16),
            vmem((16, 16, 512), BF16),
            vmem((4, 512, 256), BF16),
            vmem((4, 512, 2048), BF16),
            vmem((4, 512, 2048), BF16),
            vmem((128, 2048), BF16),
            vmem((4, 2048, 512), BF16),
            vmem((4, 512, 128), F32),
            vmem((4, 1, 512), F32),
            vmem((4, 1, 512), F32),
            vmem((8, 1, 512), F32),
            dma((100,)),
            dma((12,)),
            dma,
            dma((16, 2)),
            dma((4,)),
            dma((2,)),
            dma((2, 4)),
            dma((2,)),
            dma((4,)),
            dma((4, 4)),
            dma((4,)),
            dma((8,)),
        ],
        compiler_params=pltpu.CompilerParams(
            collective_id=0, has_side_effects=True, vmem_limit_bytes=60 * 2**20
        ),
        cost_estimate=pl.CostEstimate(flops=22 * 10**9, bytes_accessed=18 * 2**20, transcendentals=0),
        name="influence",
    )(query_grad, query_act, train_grad, train_act, basis_out, basis_in, eigenvalues)
    token_scores = scores.reshape(512)
    influence = jnp.mean(token_scores.reshape(512 // SEQ_LEN, SEQ_LEN), axis=1)
    return (token_scores, influence)


def solution(mesh):
    placed = (
        P("dp", "owner"),
        P("dp", None),
        P("dp", "owner"),
        P("dp", None),
        P("owner", None),
        P("dp", None),
        P("owner", "dp"),
    )
    return jax.shard_map(
        on_device, mesh=mesh, in_specs=placed, out_specs=(P("dp"), P("dp")), check_vma=False
    )
```

time: 300 us -> 130 us (0.43)
  waiting for transfers between devices: 189 us -> 0 us
  Pallas kernels: 0 us -> 125 us
  blocking collectives: 49.6 us -> 0 us
  matrix products: 40.1 us -> 0 us
  between operations: 14.1 us -> 0.64 us
  local copies, waits for them, and re-layouts: 6.21 us -> 1.85 us
    all_gather x2 -> x0, waiting for transfers between devices: 189 us -> none  [the longest x1 169 us: on_device(): lax.all_gather(precond, 'dp', axis=1, tiled=True)]
    pallas_call x0 -> x1, Pallas kernels: none -> 125 us  [on_device(): pl.pallas_call(kernel, out_shape=jax.ShapeDtypeStruct((1, 512), F32), in_...]
    dot_general x5 -> x0, matrix products: 40.1 us -> none  [the longest x1 25 us: on_device(): lax.dot_general(train_act, lax.all_gather(precond, 'dp', axis=1, tiled=Tr...]
    all_to_all x1 -> x0, blocking collectives: 25.6 us -> none  [on_device(): lax.all_to_all(query_act, 'dp', split_axis=1, concat_axis=0, tiled=True)]
    psum x1 -> x0, blocking collectives: 24.1 us -> none  [on_device(): scores = lax.psum(partial_value, 'owner')]
  transfers between devices with their start and end apart: 2 -> 0, of which waited for: 2 -> 0; matrix products, arithmetic and copies ran while one was open for 1% -> 0% of each run, Pallas kernels for 0% -> 0%
where the time goes in v1:
time: 130 us; the launch traced here: 129 us
  Pallas kernels  125 us (96%)
  other arithmetic  1.98 us (2%)
  local copies, waits for them, and re-layouts  1.85 us (1%)
    pallas_call x1, Pallas kernels, on_device(): pl.pallas_call(kernel, out_shape=jax.ShapeDtypeStruct((1, 512), F32), in_...  125 us

profile of v1, /device:TPU:0, one launch (start us, length us, event | category | flops | bytes accessed | tf_op | source)
XLA Modules:
  0.0 129.5 jit_solution(14522335454676974610)
XLA Ops:
  0.6 125.0 %influence.1 = f32[1,512]{1,0:T(1,128)} custom-call(bf16[64,2048]{1,0:T(8,128)(2,1)} %qg.1, bf16[64,8192]{1,0:T(8,128)(2,1)} %qa.1, bf16[512,2048]{1,0:T(8,128)(2,1)} %tg.1, bf16[512,8192]{1,0:T(8,128)(2,1)} %ta.1, bf16[2048,512]{1,0:T(8,128)(2,1)} %uo.1, bf16[512,512]{1,0:T(8,128)(2,1)} %ui.1, f32[2048,512]{1,0:T(8,128)} %lam.1), custom_call_target="tpu_custom_call" | custom-call | flops 22000001024 | bytes 18874368 | tf_op jit(solution)/shard_map/influence/pallas_call | solution.py:269
  125.6 0.5 broadcast.9
  126.1 1.3 %reduce.3 = f32[512]{0:T(512)S(1)} reduce(f32[1,512]{1,0:T(1,128)} %influence.1, f32[]{:T(128)} %broadcast.9), dimensions={0}, to_apply=%pallas_call.3.reduce_sub_computation.3 | reduce | bytes 4100 | tf_op jit(solution)/shard_map/influence/pallas_call | solution.py:269
  127.5 0.1 reshape_reshape.3
  127.6 0.1 reduce_sum.9
  127.7 0.5 broadcast_multiply_fusion
  128.2 1.3 copy.10

commit v2 on v1

--- a/solution.py
+++ b/solution.py
@@ -21,7 +21,7 @@
     return lax.dot_general(a, b, (((ca,), (cb,)), ((), ())), preferred_element_type=F32)
 
 
-def kernel(qg, qa, tg, ta, uo, ui, lam, out, qg_v, uo_v, ui_v, lam_v, rlt, gr, ac, art, gb, ab, a_st, pt, acc,
+def kernel(qg, qa, tg, ta, uo, ui, lam, out, out2, qg_v, uo_v, ui_v, lam_v, rlt, gr, ac, art, gb, ab, a_st, pt, acc,
            part, r1, r2, ssem, lsem, ac_s, gr_s, art_s, ab_s, az_s, asib_s, gsem, p_s, r1_s, r2_s):
     dp, ow = lax.axis_index("dp"), lax.axis_index("owner")
     x, yl, c = dp // 4, (dp // 2) % 2, dp % 2
@@ -66,6 +66,8 @@
     def cols(x_, yl_, c_):
         return pl.ds(pl.multiple_of(x_ * 2048 + yl_ * 1024 + c_ * 512, 512), 512)
 
+    xs = (x, xl, xr, x2)
+
     l_qg = local(qg, qg_v)
     l_uo = local(uo, uo_v)
     l_ui = local(ui, ui_v)
@@ -100,10 +102,10 @@
     z128 = pl.ds(pl.multiple_of(z * 128, 128), 128)
     for k in range(4):
         at = slice(k * 512, (k + 1) * 512)
-        send(ta.at[z128, cols(k, 1 - yl, 1 - c)], a_st.at[:, at], ab_s.at[1], bnb)
+        send(ta.at[z128, cols(xs[k], 1 - yl, 1 - c)], a_st.at[:, at], ab_s.at[1], bnb)
     for k in range(4):
         at = slice(k * 512, (k + 1) * 512)
-        send(ta.at[z128, cols(k, 1 - yl, c)], ab.at[me4, z128, at], ab_s.at[0], bnb)
+        send(ta.at[z128, cols(xs[k], 1 - yl, c)], ab.at[me4, z128, at], ab_s.at[0], bnb)
 
     def recip(k):
         rlt[k] = (1.0 / (math.sqrt(QTOK) * lam_v[k * 512:(k + 1) * 512, :])).T
@@ -119,7 +121,9 @@
         send(art.at[z], art.at[z], art_s.at[z], to)
 
     dl, dr, da = d_of(xl, yl, c), d_of(xr, yl, c), d_of(x, 1 - yl, c)
-    for h in range(2):
+    d2, dl_a, dr_a, d2_a = d_of(x2, yl, c), d_of(xl, 1 - yl, c), d_of(xr, 1 - yl, c), d_of(x2, 1 - yl, c)
+
+    def near(h):
         ggot(da, h)
         gsend(da, h, right)
         gsend(da, h, left)
@@ -131,32 +135,66 @@
             gsend(dr, h, left)
         for d in (da, dl, dr):
             gsend(d, h, sib)
-    recip(1)
-    for h in range(2):
-        d2 = d_of(x2, yl, c)
+
+    def far(h):
         ggot(d2, h)
         gsend(d2, h, across)
         gsend(d2, h, sib)
-    for h in range(2):
-        for x_ in (xl, xr):
-            d = d_of(x_, 1 - yl, c)
+
+    def rest(h):
+        for d in (dl_a, dr_a, d2_a):
             ggot(d, h)
             gsend(d, h, sib)
-    for h in range(2):
-        d = d_of(x2, 1 - yl, c)
-        ggot(d, h)
-        gsend(d, h, sib)
+
+    near(0)
+    near(1)
+    far(0)
+    recip(1)
+    far(1)
+    rest(0)
 
     send(tg, gb.at[me4], gsem.at[me4], across)
     send(tg, gb.at[me4], gsem.at[me4], sib)
     for k in range(4):
-        send(ta.at[:, cols(k, yl, 1 - c)], ab.at[me4, :, k * 512:(k + 1) * 512], asib_s.at[0], sib)
+        send(ta.at[:, cols(xs[k], yl, 1 - c)], ab.at[me4, :, k * 512:(k + 1) * 512], asib_s.at[0], sib)
     l_g = local(tg, gb.at[me4])
-    l_a = [local(ta.at[:, cols(k, yl, c)], ab.at[me4, :, k * 512:(k + 1) * 512]) for k in range(4)]
+    l_a = [local(ta.at[:, cols(xs[k], yl, c)], ab.at[me4, :, k * 512:(k + 1) * 512]) for k in range(4)]
+
+    def pre(k):
+        cross = mm(art[0], gr[k, 0].reshape(256, 512))
+        for z_ in range(1, 4):
+            cross = cross + mm(art[z_], gr[k, z_].reshape(256, 512))
+        scaled = (cross * rlt[k]).astype(BF16)
+        half = mm(scaled, uo_v[k * 512:(k + 1) * 512, :], 1, 1).astype(BF16)
+        pt[k, :512, :] = mm(ui_v[...], half).astype(BF16)
+
+    def psend(k):
+        send(pt.at[k, :512], pt.at[k, 512:1024], p_s.at[k, 0], right)
+        send(pt.at[k, :512], pt.at[k, 1024:1536], p_s.at[k, 1], left)
+
+    def sibs(h):
+        for x_ in range(4):
+            for y_ in range(2):
+                ggot(d_of(x_, y_, 1 - c), h)
+
+    for k in (1, 2, 3):
+        z_ = (z + k) % 4
+        got(art.at[z_], art_s.at[z_])
+    sibs(0)
+    pre(0)
+    psend(0)
+    rest(1)
+    pre(1)
+    psend(1)
 
     s_ac, s_ad = (1 - yl) * 2 + c, (1 - yl) * 2 + 1 - c
     got(a_st, ab_s.at[1])
     send(a_st, ab.at[s_ac, z128], asib_s.at[1], sib)
+    recip(2)
+    recip(3)
+    sibs(1)
+    pre(2)
+    pre(3)
     got(ab.at[s_ac, z128], ab_s.at[0])
     for to in zs:
         send(ab.at[s_ac, z128], ab.at[s_ac, z128], az_s.at[0, z], to)
@@ -164,92 +202,76 @@
     for to in zs:
         send(ab.at[s_ad, z128], ab.at[s_ad, z128], az_s.at[1, z], to)
 
-    recip(2)
-    recip(3)
-    for k in (1, 2, 3):
-        z_ = (z + k) % 4
-        got(art.at[z_], art_s.at[z_])
-
-    def xrows(x_):
-        return pl.ds(pl.multiple_of(x_ * 512, 512), 512)
-
-    for k in range(4):
-        if k % 2 == 0:
-            for x_ in range(4):
-                for y_ in range(2):
-                    ggot(d_of(x_, y_, 1 - c), k // 2)
-        cross = mm(art[0], gr[k, 0].reshape(256, 512))
-        for z_ in range(1, 4):
-            cross = cross + mm(art[z_], gr[k, z_].reshape(256, 512))
-        scaled = (cross * rlt[k]).astype(BF16)
-        half = mm(scaled, uo_v[k * 512:(k + 1) * 512, :], 1, 1).astype(BF16)
-        pt[k, xrows(x), :] = mm(ui_v[...], half).astype(BF16)
-        mine = pt.at[k, xrows(x)]
-        send(mine, mine, p_s.at[k, 0], right)
-        send(mine, mine, p_s.at[k, 1], left)
-
     acc[...] = jnp.zeros_like(acc)
 
-    def image(k, tb):
+    def image(k, tb, lo, hi):
         @pl.loop(0, 2)
         def _(r):
             rows = pl.ds(pl.multiple_of(r * 256, 256), 256)
-            img = mm(ab[tb, rows, :], pt[k])
+            img = mm(ab[tb, rows, lo:hi], pt[k, lo:hi, :])
             prod = img * gb[tb, rows, k * 512:(k + 1) * 512].astype(F32)
             acc[tb, rows, :] += prod[:, :128] + prod[:, 128:256] + prod[:, 256:384] + prod[:, 384:]
 
     def relay(k):
-        from_l = pt.at[k, xrows(xl)]
-        got(from_l, p_s.at[k, 0])
-        half0 = pt.at[k, pl.ds(pl.multiple_of(xl * 512, 512), 256)]
-        send(half0, half0, p_s.at[k, 2], right)
-        from_r = pt.at[k, xrows(xr)]
-        got(from_r, p_s.at[k, 1])
-        half1 = pt.at[k, pl.ds(pl.multiple_of(xr * 512 + 256, 256), 256)]
-        send(half1, half1, p_s.at[k, 3], left)
+        got(pt.at[k, 512:1024], p_s.at[k, 0])
+        send(pt.at[k, 512:768], pt.at[k, 1536:1792], p_s.at[k, 2], right)
+        got(pt.at[k, 1024:1536], p_s.at[k, 1])
+        send(pt.at[k, 1280:1536], pt.at[k, 1792:2048], p_s.at[k, 3], left)
 
     def p_all(k):
-        got(pt.at[k, pl.ds(pl.multiple_of(x2 * 512, 512), 256)], p_s.at[k, 2])
-        got(pt.at[k, pl.ds(pl.multiple_of(x2 * 512 + 256, 256), 256)], p_s.at[k, 3])
+        got(pt.at[k, 1536:1792], p_s.at[k, 2])
+        got(pt.at[k, 1792:2048], p_s.at[k, 3])
+
+    tb_own, tb_sib = me4, me4 + 1 - 2 * c
+    here, there = (tb_sib, tb_own), (s_ad, s_ac)
+    near3, far1, full = (0, 1536), (1536, 2048), (0, 2048)
+
+    def images(k, tbs, span):
+        for tb in tbs:
+            image(k, tb, *span)
 
     relay(0)
+    psend(2)
     l_g.wait()
     for cp in l_a:
         cp.wait()
-    got(gb.at[me4 + 1 - 2 * c], gsem.at[me4 + 1 - 2 * c])
-    got(ab.at[me4 + 1 - 2 * c], asib_s.at[0])
-    tb_own, tb_sib = me4, me4 + 1 - 2 * c
+    got(gb.at[tb_sib], gsem.at[tb_sib])
+    got(ab.at[tb_sib], asib_s.at[0])
+    images(0, here, near3)
     relay(1)
+    psend(3)
+    images(1, here, near3)
     p_all(0)
-    image(0, tb_own)
-    image(0, tb_sib)
+    images(0, here, far1)
     relay(2)
     got(gb.at[s_ac], gsem.at[s_ac])
     send(gb.at[s_ac], gb.at[s_ac], gsem.at[s_ac], sib)
+    images(2, here, near3)
     p_all(1)
-    image(1, tb_own)
-    image(1, tb_sib)
+    images(1, here, far1)
     for k in (1, 2, 3):
         z_ = (z + k) % 4
         rows = pl.ds(pl.multiple_of(z_ * 128, 128), 128)
         got(ab.at[s_ac, rows], az_s.at[0, z_])
         got(ab.at[s_ad, rows], az_s.at[1, z_])
     got(gb.at[s_ad], gsem.at[s_ad])
+    images(0, there, full)
+    images(1, there, full)
+    images(2, there, near3)
     relay(3)
-    for k in range(2):
-        image(k, s_ac)
-        image(k, s_ad)
-    for k in range(2, 4):
-        p_all(k)
-        for tb in (tb_own, tb_sib, s_ac, s_ad):
-            image(k, tb)
-
-    for tb in range(4):
-        part[tb] = jnp.sum(acc[tb].T, axis=0, keepdims=True)
-    for to, slot in ((sib, tb_sib), (across, s_ac), (diag, s_ad)):
-        send(part.at[slot], r1.at[me4], r1_s.at[me4], to)
-    r1[me4] = part[me4]
-    for slot in (tb_sib, s_ac, s_ad):
+    images(3, there + here, near3)
+    p_all(2)
+    images(2, there + here, far1)
+    p_all(3)
+
+    for slot, to in ((s_ad, diag), (s_ac, across), (tb_sib, sib), (tb_own, None)):
+        image(3, slot, *far1)
+        if to is None:
+            r1[slot] = jnp.sum(acc[slot].T, axis=0, keepdims=True)
+        else:
+            part[slot] = jnp.sum(acc[slot].T, axis=0, keepdims=True)
+            send(part.at[slot], r1.at[me4], r1_s.at[me4], to)
+    for slot in (s_ad, s_ac, tb_sib):
         got(r1.at[slot], r1_s.at[slot])
     r2[ow] = (r1[0] + r1[1]) + (r1[2] + r1[3])
     for to in owners:
@@ -259,18 +281,23 @@
     total = r2[0]
     for o in range(1, 8):
         total = total + r2[o]
-    out[...] = total * (1.0 / math.sqrt(DOUT * DIN))
+    total = total * (1.0 / math.sqrt(DOUT * DIN))
+    out[...] = total.reshape(512)
+    token = lax.broadcasted_iota(jnp.int32, (512, 128), 0) // SEQ_LEN
+    spread = jnp.where(token == lax.broadcasted_iota(jnp.int32, (512, 128), 1), 1.0 / SEQ_LEN, 0.0).astype(F32)
+    means = lax.dot_general(total, spread, (((1,), (0,)), ((), ())), precision=lax.Precision.HIGHEST, preferred_element_type=F32)
+    out2[...] = means.reshape(128)[:8]
     for cp in sends:
         cp.wait_send()
 
 
 def on_device(query_grad, query_act, train_grad, train_act, basis_out, basis_in, eigenvalues):
     dma, vmem = pltpu.SemaphoreType.DMA, pltpu.VMEM
-    scores = pl.pallas_call(
+    return pl.pallas_call(
         kernel,
-        out_shape=jax.ShapeDtypeStruct((1, 512), F32),
+        out_shape=(jax.ShapeDtypeStruct((512,), F32), jax.ShapeDtypeStruct((8,), F32)),
         in_specs=[pl.BlockSpec(memory_space=pl.ANY)] * 7,
-        out_specs=pl.BlockSpec(memory_space=pltpu.VMEM),
+        out_specs=(pl.BlockSpec(memory_space=pltpu.VMEM),) * 2,
         scratch_shapes=[
             vmem((64, 2048), BF16),
             vmem((2048, 512), BF16),
@@ -307,9 +334,6 @@
         cost_estimate=pl.CostEstimate(flops=22 * 10**9, bytes_accessed=18 * 2**20, transcendentals=0),
         name="influence",
     )(query_grad, query_act, train_grad, train_act, basis_out, basis_in, eigenvalues)
-    token_scores = scores.reshape(512)
-    influence = jnp.mean(token_scores.reshape(512 // SEQ_LEN, SEQ_LEN), axis=1)
-    return (token_scores, influence)
 
 
 def solution(mesh):

time: 130 us -> 115 us (0.88)
  Pallas kernels: 125 us -> 112 us
  other arithmetic: 1.98 us -> 0 us
    pallas_call x1, Pallas kernels: 125 us -> 112 us  [on_device(): pl.pallas_call(kernel, out_shape=(jax.ShapeDtypeStruct((512,), F32), jax....]
    pallas_call x1 -> x0, other arithmetic: 1.34 us -> none  [on_device(): pl.pallas_call(kernel, out_shape=jax.ShapeDtypeStruct((1, 512), F32), in_...]
where the time goes in v2:
time: 115 us
  Pallas kernels  112 us (97%)
  local copies, waits for them, and re-layouts  2.39 us (2%)
    pallas_call x1, Pallas kernels, on_device(): pl.pallas_call(kernel, out_shape=(jax.ShapeDtypeStruct((512,), F32), jax....  112 us
    unnamed x2, local copies, waits for them, and re-layouts  2.39 us

profile of v2, /device:TPU:0, one launch (start us, length us, event | category | flops | bytes accessed | tf_op | source)
XLA Modules:
  0.0 115.1 jit_solution(14932210566485636261)
XLA Ops:
  0.6 112.1 %influence.1 = (f32[512]{0:T(512)}, f32[8]{0:T(128)}) custom-call(bf16[64,2048]{1,0:T(8,128)(2,1)} %qg.1, bf16[64,8192]{1,0:T(8,128)(2,1)} %qa.1, bf16[512,2048]{1,0:T(8,128)(2,1)} %tg.1, bf16[512,8192]{1,0:T(8,128)(2,1)} %ta.1, bf16[2048,512]{1,0:T(8,128)(2,1)} %uo.1, bf16[512,512]{1,0:T(8,128)(2,1)} %ui.1, f32[2048,512]{1,0:T(8,128)} %lam.1), custom_call_target="tpu_custom_call" | custom-call | flops 22000001024 | bytes 18874368 | tf_op jit(solution)/shard_map/influence/pallas_call | solution.py:296
  112.8 1.2 %copy.11 = f32[512]{0:T(512)} copy(f32[512]{0:T(512)} %get-tuple-element.4) | data formatting | bytes 4096
  114.0 1.1 copy.12

commit v3 on v2

--- a/solution.py
+++ b/solution.py
@@ -21,7 +21,7 @@
     return lax.dot_general(a, b, (((ca,), (cb,)), ((), ())), preferred_element_type=F32)
 
 
-def kernel(qg, qa, tg, ta, uo, ui, lam, out, out2, qg_v, uo_v, ui_v, lam_v, rlt, gr, ac, art, gb, ab, a_st, pt, acc,
+def kernel(qg, qa, tg, ta, uo, ui, lam, out, out2, qa_v, qg_v, uo_v, ui_v, lam_v, rlt, gr, ac, art, gb, ab, a_st, pt, acc,
            part, r1, r2, ssem, lsem, ac_s, gr_s, art_s, ab_s, az_s, asib_s, gsem, p_s, r1_s, r2_s):
     dp, ow = lax.axis_index("dp"), lax.axis_index("owner")
     x, yl, c = dp // 4, (dp // 2) % 2, dp % 2
@@ -72,93 +72,111 @@
     l_uo = local(uo, uo_v)
     l_ui = local(ui, ui_v)
     q16 = pl.ds(pl.multiple_of(z * 16, 16), 16)
-    l_ac = local(qa.at[q16, pl.ds(pl.multiple_of(dp * 512, 512), 512)], ac.at[dp])
+    l_qa = local(qa.at[q16], qa_v)
     l_lam = local(lam, lam_v)
+
+    l_qa.wait()
+    pl.semaphore_wait(bar, len(peers))
+
+    def feats(d):
+        return pl.ds(pl.multiple_of(d * 512, 512), 512)
+
+    for to in dps:
+        send(qa_v.at[:, feats(to[1])], ac.at[dp], ac_s, to)
+
+    def gblock(d, h, part=None):
+        units = pl.ds(h, 1 + h // 2)
+        if part is None:
+            return gr.at[units, :, d]
+        return gr.at[units, :, d, :, part * 256:(part + 1) * 256]
+
+    def gsend(d, h, to, part=None):
+        send(gblock(d, h, part), gblock(d, h, part), gr_s.at[d, h, part or 0], to)
+
+    def ggot(d, h, part=None):
+        got(gblock(d, h, part), gr_s.at[d, h, part or 0])
 
     l_qg.wait()
     l_uo.wait()
-    for k in range(4):
+
+    def rotate(k):
         rot = mm(qg_v[:, k * 512:(k + 1) * 512], uo_v[k * 512:(k + 1) * 512, :])
         gr[k, :, dp, :, :] = rot.astype(BF16).reshape(4, 16, 512)
 
-    pl.semaphore_wait(bar, len(peers))
-
-    for to in dps:
-        send(qa.at[q16, pl.ds(pl.multiple_of(to[1] * 512, 512), 512)], ac.at[dp], ac_s, to)
-
-    def gblock(d, h):
-        return gr.at[pl.ds(2 * h, 2), :, d]
-
-    def gsend(d, h, to):
-        send(gblock(d, h), gblock(d, h), gr_s.at[d, h], to)
-
-    def ggot(d, h):
-        got(gblock(d, h), gr_s.at[d, h])
-
-    for h in range(2):
+    for h in range(3):
+        rotate(h)
+        if h == 2:
+            rotate(3)
         for to in (right, left, across, sib):
             gsend(dp, h, to)
+    ac[dp] = qa_v[:, feats(dp)]
 
     z128 = pl.ds(pl.multiple_of(z * 128, 128), 128)
+    for k in range(4):
+        at = slice(k * 512, (k + 1) * 512)
+        send(ta.at[z128, cols(xs[k], 1 - yl, c)], ab.at[me4, z128, at], ab_s.at[0], bnb)
+
+    def recip(k):
+        rlt[k] = (1.0 / (math.sqrt(QTOK) * lam_v[k * 512:(k + 1) * 512, :])).T
+
+
+    l_ui.wait()
+    got(ac.at[pl.ds(0, 15)], ac_s)
+    art[z] = mm(ac[...].reshape(256, 512), ui_v[...]).T.astype(BF16)
+    z_up, z_down, z_far = (z + 1) % 4, (z + 3) % 4, (z + 2) % 4
+    up, down = (yh * 4 + z_up, dp), (yh * 4 + z_down, dp)
+
+    def asend(z_, part, to):
+        rows = slice(part * 256, (part + 1) * 256)
+        send(art.at[z_, rows], art.at[z_, rows], art_s.at[z_, part], to)
+
+    def agot(z_, part):
+        got(art.at[z_, part * 256:(part + 1) * 256], art_s.at[z_, part])
+
+    asend(z, 0, up)
+    asend(z, 1, down)
+    asend(z, 1, up)
+    asend(z, 0, down)
+
+    dl, dr, da = d_of(xl, yl, c), d_of(xr, yl, c), d_of(x, 1 - yl, c)
+    d2, dl_a, dr_a, d2_a = d_of(x2, yl, c), d_of(xl, 1 - yl, c), d_of(xr, 1 - yl, c), d_of(x2, 1 - yl, c)
+
+    def ring(h):
+        ggot(dl, h)
+        gsend(dl, h, right, 0)
+        ggot(dr, h)
+        gsend(dr, h, left, 1)
+        for d in (dl, dr):
+            gsend(d, h, across)
+            gsend(d, h, sib)
+
+    ring(0)
+    l_lam.wait()
+    recip(0)
+    agot(z_down, 0)
+    asend(z_down, 0, up)
+    agot(z_up, 1)
+    asend(z_up, 1, down)
+
+    def far(h):
+        ggot(d2, h, 0)
+        ggot(d2, h, 1)
+        gsend(d2, h, across)
+        gsend(d2, h, sib)
+
+    def rest(h):
+        for d in (da, dl_a, dr_a, d2_a):
+            ggot(d, h)
+            gsend(d, h, sib)
+
+    far(0)
+    ring(1)
     for k in range(4):
         at = slice(k * 512, (k + 1) * 512)
         send(ta.at[z128, cols(xs[k], 1 - yl, 1 - c)], a_st.at[:, at], ab_s.at[1], bnb)
-    for k in range(4):
-        at = slice(k * 512, (k + 1) * 512)
-        send(ta.at[z128, cols(xs[k], 1 - yl, c)], ab.at[me4, z128, at], ab_s.at[0], bnb)
-
-    def recip(k):
-        rlt[k] = (1.0 / (math.sqrt(QTOK) * lam_v[k * 512:(k + 1) * 512, :])).T
-
-    l_lam.wait()
-    recip(0)
-
-    l_ui.wait()
-    l_ac.wait()
-    got(ac.at[pl.ds(0, 15)], ac_s)
-    art[z] = mm(ac[...].reshape(256, 512), ui_v[...]).T.astype(BF16)
-    for to in zs:
-        send(art.at[z], art.at[z], art_s.at[z], to)
-
-    dl, dr, da = d_of(xl, yl, c), d_of(xr, yl, c), d_of(x, 1 - yl, c)
-    d2, dl_a, dr_a, d2_a = d_of(x2, yl, c), d_of(xl, 1 - yl, c), d_of(xr, 1 - yl, c), d_of(x2, 1 - yl, c)
-
-    def near(h):
-        ggot(da, h)
-        gsend(da, h, right)
-        gsend(da, h, left)
-        ggot(dl, h)
-        if h == 0:
-            gsend(dl, h, right)
-        ggot(dr, h)
-        if h == 1:
-            gsend(dr, h, left)
-        for d in (da, dl, dr):
-            gsend(d, h, sib)
-
-    def far(h):
-        ggot(d2, h)
-        gsend(d2, h, across)
-        gsend(d2, h, sib)
-
-    def rest(h):
-        for d in (dl_a, dr_a, d2_a):
-            ggot(d, h)
-            gsend(d, h, sib)
-
-    near(0)
-    near(1)
-    far(0)
+    rest(0)
+    ring(2)
     recip(1)
-    far(1)
-    rest(0)
-
-    send(tg, gb.at[me4], gsem.at[me4], across)
-    send(tg, gb.at[me4], gsem.at[me4], sib)
-    for k in range(4):
-        send(ta.at[:, cols(xs[k], yl, 1 - c)], ab.at[me4, :, k * 512:(k + 1) * 512], asib_s.at[0], sib)
-    l_g = local(tg, gb.at[me4])
-    l_a = [local(ta.at[:, cols(xs[k], yl, c)], ab.at[me4, :, k * 512:(k + 1) * 512]) for k in range(4)]
 
     def pre(k):
         cross = mm(art[0], gr[k, 0].reshape(256, 512))
@@ -177,30 +195,58 @@
             for y_ in range(2):
                 ggot(d_of(x_, y_, 1 - c), h)
 
-    for k in (1, 2, 3):
-        z_ = (z + k) % 4
-        got(art.at[z_], art_s.at[z_])
+    agot(z_down, 1)
+    agot(z_up, 0)
+    agot(z_far, 0)
+    agot(z_far, 1)
     sibs(0)
     pre(0)
     psend(0)
+
+    s_ac, s_ad = (1 - yl) * 2 + c, (1 - yl) * 2 + 1 - c
+    tb_own, tb_sib = me4, me4 + 1 - 2 * c
+
+    def a_along_z(slot, which):
+        for to in zs:
+            send(ab.at[slot, z128], ab.at[slot, z128], az_s.at[which, z], to)
+
+    far(1)
+    far(2)
+    for k in range(4):
+        at = slice(k * 512, (k + 1) * 512)
+        send(tg.at[:, at], gb.at[me4, :, at], gsem.at[me4, k], across)
+    got(ab.at[s_ac, z128], ab_s.at[0])
+    a_along_z(s_ac, 0)
+    for k in range(4):
+        at = slice(k * 512, (k + 1) * 512)
+        send(tg.at[:, at], gb.at[me4, :, at], gsem.at[me4, k], sib)
+    for k in range(4):
+        send(ta.at[:, cols(xs[k], yl, 1 - c)], ab.at[me4, :, k * 512:(k + 1) * 512], asib_s.at[0], sib)
+    l_g = local(tg, gb.at[me4])
+    l_a = [local(ta.at[:, cols(xs[k], yl, c)], ab.at[me4, :, k * 512:(k + 1) * 512]) for k in range(4)]
+
+    def g_pass(k):
+        at = slice(k * 512, (k + 1) * 512)
+        got(gb.at[s_ac, :, at], gsem.at[s_ac, k])
+        send(gb.at[s_ac, :, at], gb.at[s_ac, :, at], gsem.at[s_ac, k], sib)
+
+    def g_got(slot, k):
+        got(gb.at[slot, :, k * 512:(k + 1) * 512], gsem.at[slot, k])
+
     rest(1)
+    sibs(1)
     pre(1)
     psend(1)
-
-    s_ac, s_ad = (1 - yl) * 2 + c, (1 - yl) * 2 + 1 - c
     got(a_st, ab_s.at[1])
     send(a_st, ab.at[s_ac, z128], asib_s.at[1], sib)
     recip(2)
     recip(3)
-    sibs(1)
+    rest(2)
+    sibs(2)
     pre(2)
     pre(3)
-    got(ab.at[s_ac, z128], ab_s.at[0])
-    for to in zs:
-        send(ab.at[s_ac, z128], ab.at[s_ac, z128], az_s.at[0, z], to)
     got(ab.at[s_ad, z128], asib_s.at[1])
-    for to in zs:
-        send(ab.at[s_ad, z128], ab.at[s_ad, z128], az_s.at[1, z], to)
+    a_along_z(s_ad, 1)
 
     acc[...] = jnp.zeros_like(acc)
 
@@ -222,7 +268,6 @@
         got(pt.at[k, 1536:1792], p_s.at[k, 2])
         got(pt.at[k, 1792:2048], p_s.at[k, 3])
 
-    tb_own, tb_sib = me4, me4 + 1 - 2 * c
     here, there = (tb_sib, tb_own), (s_ad, s_ac)
     near3, far1, full = (0, 1536), (1536, 2048), (0, 2048)
 
@@ -235,17 +280,18 @@
     l_g.wait()
     for cp in l_a:
         cp.wait()
-    got(gb.at[tb_sib], gsem.at[tb_sib])
+    for k in range(4):
+        g_got(tb_sib, k)
     got(ab.at[tb_sib], asib_s.at[0])
     images(0, here, near3)
     relay(1)
     psend(3)
+    g_pass(0)
     images(1, here, near3)
     p_all(0)
     images(0, here, far1)
+    g_pass(1)
     relay(2)
-    got(gb.at[s_ac], gsem.at[s_ac])
-    send(gb.at[s_ac], gb.at[s_ac], gsem.at[s_ac], sib)
     images(2, here, near3)
     p_all(1)
     images(1, here, far1)
@@ -254,14 +300,19 @@
         rows = pl.ds(pl.multiple_of(z_ * 128, 128), 128)
         got(ab.at[s_ac, rows], az_s.at[0, z_])
         got(ab.at[s_ad, rows], az_s.at[1, z_])
-    got(gb.at[s_ad], gsem.at[s_ad])
+    g_pass(2)
+    g_got(s_ad, 0)
     images(0, there, full)
+    g_pass(3)
+    relay(3)
+    g_got(s_ad, 1)
     images(1, there, full)
+    g_got(s_ad, 2)
     images(2, there, near3)
-    relay(3)
+    p_all(2)
+    images(2, here + there, far1)
+    g_got(s_ad, 3)
     images(3, there + here, near3)
-    p_all(2)
-    images(2, there + here, far1)
     p_all(3)
 
     for slot, to in ((s_ad, diag), (s_ac, across), (tb_sib, sib), (tb_own, None)):
@@ -299,6 +350,7 @@
         in_specs=[pl.BlockSpec(memory_space=pl.ANY)] * 7,
         out_specs=(pl.BlockSpec(memory_space=pltpu.VMEM),) * 2,
         scratch_shapes=[
+            vmem((16, 8192), BF16),
             vmem((64, 2048), BF16),
             vmem((2048, 512), BF16),
             vmem((512, 512), BF16),
@@ -315,15 +367,15 @@
             vmem((4, 1, 512), F32),
             vmem((4, 1, 512), F32),
             vmem((8, 1, 512), F32),
-            dma((100,)),
+            dma((140,)),
             dma((12,)),
             dma,
-            dma((16, 2)),
-            dma((4,)),
+            dma((16, 3, 2)),
+            dma((4, 2)),
             dma((2,)),
             dma((2, 4)),
             dma((2,)),
-            dma((4,)),
+            dma((4, 4)),
             dma((4, 4)),
             dma((4,)),
             dma((8,)),

time: 115 us -> 113 us (0.983)
  Pallas kernels: 112 us -> 110 us
    pallas_call x1, Pallas kernels: 112 us -> 110 us  [on_device(): pl.pallas_call(kernel, out_shape=(jax.ShapeDtypeStruct((512,), F32), jax....]
where the time goes in v3:
time: 113 us
  Pallas kernels  110 us (97%)
  local copies, waits for them, and re-layouts  2.39 us (2%)
    pallas_call x1, Pallas kernels, on_device(): pl.pallas_call(kernel, out_shape=(jax.ShapeDtypeStruct((512,), F32), jax....  110 us
    unnamed x2, local copies, waits for them, and re-layouts  2.39 us

profile of v3, /device:TPU:0, one launch (start us, length us, event | category | flops | bytes accessed | tf_op | source)
XLA Modules:
  0.0 113.3 jit_solution(16066402339036472711)
XLA Ops:
  0.6 110.3 %influence.1 = (f32[512]{0:T(512)}, f32[8]{0:T(128)}) custom-call(bf16[64,2048]{1,0:T(8,128)(2,1)} %qg.1, bf16[64,8192]{1,0:T(8,128)(2,1)} %qa.1, bf16[512,2048]{1,0:T(8,128)(2,1)} %tg.1, bf16[512,8192]{1,0:T(8,128)(2,1)} %ta.1, bf16[2048,512]{1,0:T(8,128)(2,1)} %uo.1, bf16[512,512]{1,0:T(8,128)(2,1)} %ui.1, f32[2048,512]{1,0:T(8,128)} %lam.1), custom_call_target="tpu_custom_call" | custom-call | flops 22000001024 | bytes 18874368 | tf_op jit(solution)/shard_map/influence/pallas_call | solution.py:347
  110.9 1.2 %copy.11 = f32[512]{0:T(512)} copy(f32[512]{0:T(512)} %get-tuple-element.4) | data formatting | bytes 4096
  112.2 1.1 %copy.12 = f32[8]{0:T(128)} copy(f32[8]{0:T(128)} %get-tuple-element.5) | data formatting | bytes 64

commit v4 on v3

--- a/solution.py
+++ b/solution.py
@@ -303,16 +303,17 @@
     g_pass(2)
     g_got(s_ad, 0)
     images(0, there, full)
-    g_pass(3)
-    relay(3)
     g_got(s_ad, 1)
     images(1, there, full)
+    relay(3)
+    g_pass(3)
     g_got(s_ad, 2)
     images(2, there, near3)
+    images(3, here, near3)
+    g_got(s_ad, 3)
+    images(3, there, near3)
     p_all(2)
     images(2, here + there, far1)
-    g_got(s_ad, 3)
-    images(3, there + here, near3)
     p_all(3)
 
     for slot, to in ((s_ad, diag), (s_ac, across), (tb_sib, sib), (tb_own, None)):

time: 113 us -> 111 us (0.982)
  Pallas kernels: 110 us -> 108 us
    pallas_call x1, Pallas kernels: 110 us -> 108 us  [on_device(): pl.pallas_call(kernel, out_shape=(jax.ShapeDtypeStruct((512,), F32), jax....]
where the time goes in v4:
time: 111 us
  Pallas kernels  108 us (97%)
  local copies, waits for them, and re-layouts  2.39 us (2%)
    pallas_call x1, Pallas kernels, on_device(): pl.pallas_call(kernel, out_shape=(jax.ShapeDtypeStruct((512,), F32), jax....  108 us
    unnamed x2, local copies, waits for them, and re-layouts  2.39 us

profile of v4, /device:TPU:0, one launch (start us, length us, event | category | flops | bytes accessed | tf_op | source)
XLA Modules:
  0.0 111.4 jit_solution(2144258667529311807)
XLA Ops:
  0.6 108.3 %influence.1 = (f32[512]{0:T(512)}, f32[8]{0:T(128)}) custom-call(bf16[64,2048]{1,0:T(8,128)(2,1)} %qg.1, bf16[64,8192]{1,0:T(8,128)(2,1)} %qa.1, bf16[512,2048]{1,0:T(8,128)(2,1)} %tg.1, bf16[512,8192]{1,0:T(8,128)(2,1)} %ta.1, bf16[2048,512]{1,0:T(8,128)(2,1)} %uo.1, bf16[512,512]{1,0:T(8,128)(2,1)} %ui.1, f32[2048,512]{1,0:T(8,128)} %lam.1), custom_call_target="tpu_custom_call" | custom-call | flops 22000001024 | bytes 18874368 | tf_op jit(solution)/shard_map/influence/pallas_call | solution.py:348
  109.0 1.2 %copy.11 = f32[512]{0:T(512)} copy(f32[512]{0:T(512)} %get-tuple-element.4) | data formatting | bytes 4096
  110.2 1.1 %copy.12 = f32[8]{0:T(128)} copy(f32[8]{0:T(128)} %get-tuple-element.5) | data formatting | bytes 64
